TPU v7x, 256 devices: a whole 4x4x8 slice. The times are simulated.
256 devices in a mesh: ctx: 64 (over z, x, core), head: 4 (over y).
Axes of the slice: x: 4, y: 4, z: 8, core: 2. Of those that a mesh axis runs over, the one named last changes fastest.
Arguments:
- queries: bfloat16 [16384, 2560], P('ctx', 'head'), may hold values from -5 to 5
- keys: bfloat16 [16384, 512], P('ctx', 'head'), may hold values from -4.5 to 4.5
- values: bfloat16 [16384, 512], P('ctx', 'head'), may hold values from -6 to 6
- token_types: int32 [16384], P('ctx'), may hold values 0 or 1
- type_bias: float32 [20, 2, 2], P('head'), may hold values from -2 to 2
- out_weight: bfloat16 [2560, 5120], P('head'), may hold values from -0.125 to 0.125
Outputs:
- mixed: bfloat16 [16384, 5120], P('ctx', 'head')
All inputs are finite; a program needn't handle non-finite values. No bound on the sum of `token_types` on one device may be relied on, other than what follows from the above.
Results may differ from a plain program's by a relative error of at most 0.013.
Values may be sent and summed in bfloat16 or wider, within the bound.
No kernel may reach another device: no remote copies, remote signals or barrier semaphores. Data moves between devices by JAX's collectives and lax.ppermute only.
A program may use at most 128 MiB of HBM per device.

v0:
```python
import functools
import math

import jax
import jax.numpy as jnp
from jax import lax
from jax.experimental import pallas as pl
from jax.experimental.pallas import tpu as pltpu
from jax.sharding import Mesh, PartitionSpec as P

f32 = jnp.float32
bf16 = jnp.bfloat16
HEAD = 128
EXTRA = 16
SUM_ROWS = 8
ACC_ROWS = HEAD + SUM_ROWS
STATE_ROWS = ACC_ROWS + 8
MASKED = -1e30
ROOM = 64.0
VMEM_LIMIT = 12 * 2**20
SMALL_LIMIT = 8 * 2**20
LOG2_SCALE = 1.4426950408889634 / math.sqrt(HEAD)


def stage_keys(blocks, first, keys_ref, values_ref):
    block = blocks[0].shape[0] - EXTRA
    row = lax.broadcasted_iota(jnp.int32, (EXTRA, HEAD), 0)
    col = lax.broadcasted_iota(jnp.int32, (EXTRA, HEAD), 1)
    spread = jnp.where((row < 2) & (col < 6) & (col % 2 == row), 1.0, 0.0).astype(bf16)
    for number, msg in enumerate(blocks):
        at = first + number * block
        keys_ref[at : at + block, :HEAD] = msg[:block, :HEAD]
        marks = lax.dot_general(
            msg[block:, :], spread, (((0,), (0,)), ((), ())), preferred_element_type=f32
        )
        keys_ref[at : at + block, HEAD:] = marks.astype(bf16)
        for part in range(block // HEAD):
            rows = slice(part * HEAD, (part + 1) * HEAD)
            cols = slice(at + part * HEAD, at + (part + 1) * HEAD)
            values_ref[:HEAD, cols] = msg[rows, HEAD:]
    total = len(blocks) * block
    values_ref[HEAD:, first : first + total] = jnp.ones((SUM_ROWS, total), bf16)


def blocks_of(refs):
    blocks = []
    for ref in refs:
        blocks += [ref] if len(ref.shape) == 2 else [ref.at[i] for i in range(ref.shape[0])]
    return blocks


def score(keys, queries):
    return lax.dot_general(keys, queries, (((1,), (1,)), ((), ())), preferred_element_type=f32)


def prepare_keys_kernel(keys_ref, values_ref, kind_ref, out_ref, token_ref):
    token_ref[0] = 0
    block = keys_ref.shape[0]
    out_ref[:block, :HEAD] = keys_ref[...]
    for at in range(0, block, HEAD):
        turned = values_ref[at : at + HEAD, :].astype(f32).T
        out_ref[at : at + HEAD, HEAD:] = turned.astype(bf16)
    out_ref[block:, :] = type_marks(kind_ref)


def type_marks(kind_ref):
    kinds = jnp.broadcast_to(kind_ref[...].astype(f32), (EXTRA, kind_ref.shape[1]))
    row = lax.broadcasted_iota(jnp.int32, kinds.shape, 0)
    return jnp.where(row == 0, 1.0 - kinds, jnp.where(row == 1, kinds, 0.0)).astype(bf16)


def prepare_queries_kernel(bias_ref, query_ref, kind_ref, gate_ref, out_ref, token_ref):
    token_ref[0] = 0
    marks = type_marks(kind_ref)
    row = lax.broadcasted_iota(jnp.int32, (EXTRA, HEAD), 0)
    col = lax.broadcasted_iota(jnp.int32, (EXTRA, HEAD), 1)
    for head in range(out_ref.shape[0]):
        out_ref[head, :, :HEAD] = query_ref[:, head * HEAD : (head + 1) * HEAD]
        pairs = [bias_ref[4 * head + i] * math.sqrt(HEAD) for i in range(4)]
        first = jnp.where(col % 2 == 0, pairs[0], pairs[1])
        second = jnp.where(col % 2 == 0, pairs[2], pairs[3])
        table = jnp.where(row == 0, first, jnp.where(row == 1, second, 0.0))
        high = table.astype(bf16)
        rest = table - high.astype(f32)
        middle = rest.astype(bf16)
        low = (rest - middle.astype(f32)).astype(bf16)
        group = col // 2
        terms = jnp.where(
            group == 0,
            high.astype(f32),
            jnp.where(group == 1, middle.astype(f32), jnp.where(group == 2, low.astype(f32), 0.0)),
        ).astype(bf16)
        spread = lax.dot_general(
            marks, terms, (((0,), (0,)), ((), ())), preferred_element_type=f32
        )
        out_ref[head, :, HEAD:] = spread.astype(bf16)


def own_kernel(msgs, where_ref, mine_ref, other_ref, *refs):
    state_ref, token_ref, keys_ref, values_ref = refs[msgs:]
    blocks = blocks_of(refs[:msgs])
    slots = len(blocks)
    heads, block, _ = mine_ref.shape
    lanes = 2 * block
    stage_keys(blocks, 0, keys_ref, values_ref)
    token_ref[0] = where_ref[0] * 0
    lane = lax.broadcasted_iota(jnp.int32, (block, lanes), 1)
    query_pos = jnp.where(lane < block, where_ref[0] + lane, where_ref[1] + lane - block)
    ahead = lax.broadcasted_iota(jnp.int32, (block, lanes), 0) - query_pos

    def one_head(head, carry):
        queries = jnp.concatenate([mine_ref[head], other_ref[head]], axis=0)
        at = pl.ds(pl.multiple_of(head * lanes, HEAD), lanes)
        peak = jnp.full((1, lanes), MASKED, f32)
        parts = []
        for slot in range(slots):
            piece = score(keys_ref[slot * block : (slot + 1) * block, :], queries)
            piece = jnp.where(ahead <= -where_ref[2 + slot], piece, MASKED)
            peak = jnp.maximum(peak, jnp.max(piece, axis=0, keepdims=True))
            parts.append(piece)
        peak = jnp.where(peak > 0.5 * MASKED, peak, 0.0)
        shift = peak * LOG2_SCALE
        weights = jnp.concatenate(
            [jnp.exp2(part * LOG2_SCALE - shift).astype(bf16) for part in parts], axis=0
        )
        state_ref[:ACC_ROWS, at] = jnp.dot(values_ref[...], weights, preferred_element_type=f32)
        state_ref[ACC_ROWS:, at] = jnp.broadcast_to(peak, (8, lanes))
        return carry

    lax.fori_loop(0, heads, one_head, 0)


def add_keys(
    count, mine_ref, other_ref, keys_ref, values_ref, size, old_ref, state_ref, unroll
):
    heads, block, _ = mine_ref.shape
    lanes = 2 * block
    state_ref[...] = old_ref[...]

    def queries_of(head):
        return jnp.concatenate([mine_ref[head], other_ref[head]], axis=0)

    def lanes_of(head):
        return pl.ds(pl.multiple_of(head * lanes, HEAD), lanes)

    def unit(step, worst):
        head, plane = step % heads, step // heads
        at = lanes_of(head)
        part = pl.ds(pl.multiple_of(plane * size, size), size)
        peak = old_ref[ACC_ROWS : ACC_ROWS + 1, at]
        mass = old_ref[HEAD : HEAD + 1, at]
        scores = score(keys_ref[part, :], queries_of(head))
        top = jnp.max(scores, axis=0, keepdims=True)
        weights = jnp.exp2(scores * LOG2_SCALE - peak * LOG2_SCALE).astype(bf16)
        state_ref[:ACC_ROWS, at] += jnp.dot(
            values_ref[:, part], weights, preferred_element_type=f32
        )
        rise = (top - peak) * LOG2_SCALE
        bad = (rise > ROOM) | ((mass <= 0.0) & (rise < -ROOM))
        return jnp.maximum(worst, jnp.where(bad, 1.0, 0.0))

    def units(turn, worst):
        for part in range(unroll):
            worst = unit(turn * unroll + part, worst)
        return worst

    turns = count * (heads // unroll)
    worst = lax.fori_loop(0, turns, units, jnp.zeros((1, lanes), f32))

    @pl.when(jnp.max(worst) > 0.5)
    def _():
        state_ref[...] = old_ref[...]
        step_rows = 128
        chunks = size // step_rows

        def redo(step, carry):
            at = lanes_of(step % heads)
            part = pl.ds(pl.multiple_of((step // heads) * step_rows, step_rows), step_rows)
            peak = state_ref[ACC_ROWS : ACC_ROWS + 1, at]
            mass = state_ref[HEAD : HEAD + 1, at]
            scores = score(keys_ref[part, :], queries_of(step % heads))
            top = jnp.max(scores, axis=0, keepdims=True)
            fresh = jnp.where(mass > 0.0, jnp.maximum(peak, top), top)
            fade = jnp.where(mass > 0.0, jnp.exp2((peak - fresh) * LOG2_SCALE), 0.0)
            weights = jnp.exp2(scores * LOG2_SCALE - fresh * LOG2_SCALE).astype(bf16)
            update = jnp.dot(values_ref[:, part], weights, preferred_element_type=f32)
            state_ref[:ACC_ROWS, at] = state_ref[:ACC_ROWS, at] * fade + update
            state_ref[ACC_ROWS:, at] = jnp.broadcast_to(fresh, (8, lanes))
            return carry

        lax.fori_loop(0, heads * count * chunks, redo, 0)


def plane_kernel(plan, last, gates, count_ref, mine_ref, other_ref, *refs):
    msgs = 1 + max(index for plane in plan for index, _ in plane)
    old_ref = refs[msgs]
    if last:
        kept_ref, parcel_ref, token_ref, state_ref, keys_ref, values_ref = refs[msgs + 1 + gates :]
    else:
        state_ref, token_ref, keys_ref, values_ref = refs[msgs + 1 + gates :]
    blocks = [blocks_of([ref]) for ref in refs[:msgs]]
    heads, block, _ = mine_ref.shape
    size = len(plan[0]) * block
    count = count_ref[0]
    for number, plane in enumerate(plan):

        @pl.when(count > number)
        def _(number=number, plane=plane):
            stage_keys([blocks[i][j] for i, j in plane], number * size, keys_ref, values_ref)

    unroll = 1 if last else heads
    add_keys(count, mine_ref, other_ref, keys_ref, values_ref, size, old_ref, state_ref, unroll)
    token_ref[0] = count * 0
    if not last:
        return
    for head in range(heads):
        finish(block, head, state_ref, kept_ref.at[head], parcel_ref.at[head])


def finish(block, head, state_ref, kept_ref, parcel_ref):
    at = slice(head * 2 * block, (head + 1) * 2 * block)
    mass = state_ref[HEAD : HEAD + 1, at]
    peak = state_ref[ACC_ROWS : ACC_ROWS + 1, at]
    full = mass > 0.0
    safe = jnp.where(full, mass, 1.0)
    level = jnp.where(full, peak * LOG2_SCALE + jnp.log2(safe), MASKED)
    mean = state_ref[:HEAD, at] * (1.0 / safe)
    kept_ref[:HEAD, :] = mean[:, :block]
    kept_ref[HEAD:, :] = jnp.broadcast_to(level[:, :block], (8, block))
    parcel_ref[:HEAD, :] = mean[:, block:].astype(bf16)
    whole = jnp.broadcast_to(level[:, block:], (EXTRA, block))
    high = whole.astype(bf16)
    rest = whole - high.astype(f32)
    middle = rest.astype(bf16)
    low = rest - middle.astype(f32)
    row = lax.broadcasted_iota(jnp.int32, whole.shape, 0)
    parcel_ref[HEAD:, :] = jnp.where(
        row == 0,
        high.astype(f32),
        jnp.where(row == 1, middle.astype(f32), jnp.where(row == 2, low, 0.0)),
    ).astype(bf16)


def merge_kernel(kept_ref, came_ref, low_ref, high_ref, token_ref):
    token_ref[0] = 0
    half = low_ref.shape[0]
    for head in range(kept_ref.shape[0]):
        kept_level = kept_ref[head, HEAD : HEAD + 1, :]
        extra = came_ref[head, HEAD:, :].astype(f32)
        came_level = extra[0:1] + extra[1:2] + extra[2:3]
        top = jnp.maximum(kept_level, came_level)
        kept_part = jnp.exp2(kept_level - top)
        came_part = jnp.exp2(came_level - top)
        share = 1.0 / (kept_part + came_part)
        mixed = kept_ref[head, :HEAD, :] * (kept_part * share) + came_ref[head, :HEAD, :].astype(
            f32
        ) * (came_part * share)
        cols = slice(head * HEAD, (head + 1) * HEAD)
        low_ref[:, cols] = mixed[:, :half].T.astype(bf16)
        high_ref[:, cols] = mixed[:, half:].T.astype(bf16)


def whole(value):
    return pl.BlockSpec(value.shape, lambda *_: (0,) * value.ndim)


IN_VMEM = pl.BlockSpec(memory_space=pltpu.VMEM)
IN_SMEM = pl.BlockSpec(memory_space=pltpu.SMEM)


def attend_own(where, mine, other, msgs):
    heads, block, depth = mine.shape
    lanes = 2 * block
    total = block * sum(1 if m.ndim == 2 else m.shape[0] for m in msgs)
    return pl.pallas_call(
        functools.partial(own_kernel, len(msgs)),
        in_specs=[IN_SMEM] + [IN_VMEM] * (2 + len(msgs)),
        out_specs=[IN_VMEM, IN_SMEM],
        scratch_shapes=[pltpu.VMEM((total, 2 * HEAD), bf16), pltpu.VMEM((ACC_ROWS, total), bf16)],
        out_shape=[
            jax.ShapeDtypeStruct((STATE_ROWS, heads * lanes), f32),
            jax.ShapeDtypeStruct((1,), jnp.int32),
        ],
        compiler_params=pltpu.CompilerParams(vmem_limit_bytes=VMEM_LIMIT),
        cost_estimate=pl.CostEstimate(
            flops=8 * heads * lanes * total * 256, bytes_accessed=2**20, transcendentals=0
        ),
        name="own_plane",
    )(where, mine, other, *msgs)


def attend_planes(count, mine, other, msgs, plan, state, last=False, gates=()):
    heads, block, depth = mine.shape
    lanes = 2 * block
    total = block * sum(len(plane) for plane in plan)
    scratch = [pltpu.VMEM((total, 2 * HEAD), bf16), pltpu.VMEM((ACC_ROWS, total), bf16)]
    if last:
        out_specs = [IN_VMEM, IN_VMEM, IN_SMEM]
        out_shape = [
            jax.ShapeDtypeStruct((heads, ACC_ROWS, block), f32),
            jax.ShapeDtypeStruct((heads, STATE_ROWS, block), bf16),
            jax.ShapeDtypeStruct((1,), jnp.int32),
        ]
        scratch = [pltpu.VMEM((STATE_ROWS, heads * lanes), f32)] + scratch
    else:
        out_specs = [IN_VMEM, IN_SMEM]
        out_shape = [
            jax.ShapeDtypeStruct((STATE_ROWS, heads * lanes), f32),
            jax.ShapeDtypeStruct((1,), jnp.int32),
        ]
    return pl.pallas_call(
        functools.partial(plane_kernel, plan, last, len(gates)),
        in_specs=[IN_SMEM]
        + [IN_VMEM] * (3 + len(msgs))
        + [pl.BlockSpec(memory_space=pl.ANY)] * len(gates),
        out_specs=out_specs,
        scratch_shapes=scratch,
        out_shape=out_shape,
        compiler_params=pltpu.CompilerParams(vmem_limit_bytes=VMEM_LIMIT),
        cost_estimate=pl.CostEstimate(
            flops=6 * heads * lanes * total * 256, bytes_accessed=2**20, transcendentals=0
        ),
        name="last_planes" if last else "planes",
    )(count, mine, other, *msgs, state, *gates)


def joined(pair):
    return jnp.concatenate([pair[0][...], pair[1][...]], axis=0)


def near_kernel(core_ref, own, below, above, own_w, up_w, down_w, out_ref):
    rows, width = up_w[0].shape
    out_ref[...] = jnp.dot(joined(own), own_w[...], preferred_element_type=f32)
    low, high = joined(below), joined(above)
    for side in range(2):
        first = jnp.where(core_ref[0] == side, 0, width)
        at = pl.ds(pl.multiple_of(first, HEAD), width)
        more = jnp.dot(low, up_w[side][...], preferred_element_type=f32)
        out_ref[:, at] += more + jnp.dot(high, down_w[side][...], preferred_element_type=f32)


def far_kernel(core_ref, near_ref, pair, far_w, out_ref):
    part = joined(pair)
    width = far_w[0].shape[1]
    for side in range(2):
        first = jnp.where(core_ref[0] == side, 0, width)
        at = pl.ds(pl.multiple_of(first, HEAD), width)
        more = jnp.dot(part, far_w[side][...], preferred_element_type=f32)
        out_ref[:, at] = (near_ref[:, at] + more).astype(bf16)


def project_near(core, own, below, above, own_w, up_w, down_w):
    block, cols = 2 * own[0].shape[0], own_w.shape[1]
    pair = [IN_VMEM] * 2
    return pl.pallas_call(
        near_kernel,
        in_specs=[IN_SMEM, pair, pair, pair, IN_VMEM, pair, pair],
        out_specs=IN_VMEM,
        out_shape=jax.ShapeDtypeStruct((block, cols), f32),
        compiler_params=pltpu.CompilerParams(vmem_limit_bytes=VMEM_LIMIT),
        name="project_near",
    )(core, list(own), below, above, own_w, up_w, down_w)


def project_far(core, near, opposite, far_w):
    pair = [IN_VMEM] * 2
    return pl.pallas_call(
        far_kernel,
        in_specs=[IN_SMEM, IN_VMEM, pair, pair],
        out_specs=IN_VMEM,
        out_shape=jax.ShapeDtypeStruct(near.shape, bf16),
        compiler_params=pltpu.CompilerParams(vmem_limit_bytes=VMEM_LIMIT),
        name="project_far",
    )(core, near, opposite, far_w)


def carve_kernel(column_ref, weight_ref, out_ref, sem):
    column = pl.multiple_of(column_ref[0], HEAD)
    copy = pltpu.make_async_copy(weight_ref.at[:, pl.ds(column, out_ref.shape[1])], out_ref, sem)
    copy.start()
    copy.wait()


def take_columns(column, weight, width):
    rows = weight.shape[0]
    return pl.pallas_call(
        carve_kernel,
        in_specs=[IN_SMEM, pl.BlockSpec(memory_space=pltpu.HBM)],
        out_specs=IN_VMEM,
        out_shape=jax.ShapeDtypeStruct((rows, width), weight.dtype),
        scratch_shapes=[pltpu.SemaphoreType.DMA],
        compiler_params=pltpu.CompilerParams(vmem_limit_bytes=SMALL_LIMIT),
        name="carve",
    )(column, weight)


def shift(value, axis, size, step):
    return lax.ppermute(value, axis, [(i, (i + step) % size) for i in range(size)])


def with_sibling(weight, token):
    weight = weight + token[0].astype(bf16)
    return [weight, shift(weight, "core", 2, 1)]


def shards(sizes, queries, keys, values, token_types, type_bias, out_weight):
    nz, nx, nc, ny = sizes
    zi, xi, ci, yi = (lax.axis_index(a) for a in ("z", "x", "core", "head"))
    block = queries.shape[0]
    heads = type_bias.shape[0]
    kinds = token_types.reshape(1, block)

    message, early = pl.pallas_call(
        prepare_keys_kernel,
        out_specs=[IN_VMEM, IN_SMEM],
        out_shape=[
            jax.ShapeDtypeStruct((block + EXTRA, 2 * HEAD), bf16),
            jax.ShapeDtypeStruct((1,), jnp.int32),
        ],
        name="prepare_keys",
    )(keys, values, kinds)

    across = shift(message, "x", nx, 2)
    right = shift(message, "x", nx, 1)
    left = shift(message, "x", nx, -1)
    plane = jnp.stack([message, right, across, left])
    mine, ready = pl.pallas_call(
        prepare_queries_kernel,
        in_specs=[IN_SMEM] + [IN_VMEM] * 3,
        out_specs=[IN_VMEM, IN_SMEM],
        out_shape=[
            jax.ShapeDtypeStruct((heads, block, 2 * HEAD), bf16),
            jax.ShapeDtypeStruct((1,), jnp.int32),
        ],
        name="prepare_queries",
    )(type_bias.reshape(-1), queries, kinds, plane)
    other = shift(mine, "core", nc, 1)

    forward, backward = [plane], [plane]

    def onward(token):
        zero = 0 if token is None else token[0].astype(bf16)
        forward.append(shift(forward[-1] + zero, "z", nz, 1))
        backward.append(shift(backward[-1] + zero, "z", nz, -1))

    onward(None)

    rows_w, cols_w = out_weight.shape[0], out_weight.shape[1] // ny
    half = cols_w // nc

    def column(step):
        return ((yi + step) % ny) * cols_w + ci * half

    up_w, down_w = [
        shift(
            lax.dynamic_slice(out_weight, (0, column(step) + ready[0]), (rows_w, half)),
            "head",
            ny,
            step,
        )
        for step in (1, -1)
    ]

    chip = (zi * nx + xi) * nc
    homes = [((zi * nx + (xi - d) % nx) * nc + ci) * block for d in range(nx)]
    where = jnp.stack([(chip + ci) * block, (chip + 1 - ci) * block] + homes).astype(jnp.int32)
    state, token = attend_own(where, mine, other, [plane])
    far_w = shift(
        take_columns((column(2) + token).astype(jnp.int32), out_weight, half), "head", ny, 2
    )
    onward(token)
    onward(None)
    far_parts = [forward[3][: nx // 2], backward[3][nx // 2 :]]
    far = [shift(far_parts[0], "z", nz, 1), shift(far_parts[1], "z", nz, -1)]
    planes = tuple(tuple((i, j) for j in range(nx)) for i in range(2))
    for step in (1, 2, 3):
        count = jnp.stack([jnp.where(zi >= nz - step, 2, jnp.where(zi >= step, 1, 0))])
        state, token = attend_planes(
            count.astype(jnp.int32),
            mine,
            other,
            [forward[step], backward[step]],
            planes,
            state,
            gates=far_parts if step == 3 else (),
        )
        if step == 2:
            up_w, down_w = with_sibling(up_w, token), with_sibling(down_w, token)
    count = jnp.stack([jnp.where(zi >= nz // 2, 1, 0)]).astype(jnp.int32)
    kept, parcel, token = attend_planes(
        count, mine, other, far, (((0, 0), (0, 1), (1, 0), (1, 1)),), state, last=True
    )

    came = shift(parcel, "core", nc, 1)
    *own, merged = pl.pallas_call(
        merge_kernel,
        out_specs=[IN_VMEM, IN_VMEM, IN_SMEM],
        out_shape=[jax.ShapeDtypeStruct((block // 2, heads * HEAD), bf16)] * 2
        + [jax.ShapeDtypeStruct((1,), jnp.int32)],
        compiler_params=pltpu.CompilerParams(vmem_limit_bytes=SMALL_LIMIT),
        name="merge",
    )(kept, came)

    below = [shift(own[0], "head", ny, 1), None]
    above = [None, shift(own[1], "head", ny, -1)]
    below[1] = shift(own[1], "head", ny, 1)
    above[0] = shift(own[0], "head", ny, -1)
    opposite = [shift(below[0], "head", ny, 1), shift(above[1], "head", ny, -1)]
    own_w = lax.dynamic_slice(out_weight, (0, yi * cols_w + token[0]), (rows_w, cols_w))
    core = jnp.stack([ci]).astype(jnp.int32)
    near = project_near(core, own, below, above, own_w, up_w, down_w)
    return project_far(core, near, opposite, with_sibling(far_w, merged))


def solution(mesh):
    nz, nx, nc, ny = 8, 4, 2, 4
    grid = Mesh(mesh.devices.reshape(nz, nx, nc, ny), ("z", "x", "core", "head"))
    ctx = ("z", "x", "core")
    in_specs = (
        P(ctx, "head"),
        P(ctx, "head"),
        P(ctx, "head"),
        P(ctx),
        P("head", None, None),
        P("head", None),
    )
    return jax.shard_map(
        functools.partial(shards, (nz, nx, nc, ny)),
        mesh=grid,
        in_specs=in_specs,
        out_specs=P(ctx, "head"),
        check_vma=False,
    )
```

profile of v0, /device:TPU:224, one launch (start us, length us, event | category | flops | bytes accessed | tf_op | source)
XLA Modules:
  0.0 129.1 jit_solution(16607445180181922733)
XLA Ops:
  1.7 2.8 %collective-permute-start.2 = (bf16[272,256]{1,0:T(8,128)(2,1)}, bf16[272,256]{1,0:T(8,128)(2,1)S(1)}, u32[]{:S(2)}, u32[]{:S(2)}) collective-permute-start(bf16[272,256]{1,0:T(8,128)(2,1)} %get-tuple-element.20), channel_id=1, source_target_pairs={{0,24},{8,0},{16,8},{24,16},{1,25},{9,1},{17,9},{25,17},{2,26},{10... | collective-permute-start | bytes 417800 | tf_op jit(solution)/shard_map/ppermute | solution.py:398
  7.6 3.2 %collective-permute-done.2 = bf16[272,256]{1,0:T(8,128)(2,1)S(1)} collective-permute-done((bf16[272,256]{1,0:T(8,128)(2,1)}, bf16[272,256]{1,0:T(8,128)(2,1)S(1)}, u32[]{:S(2)}, u32[]{:S(2)}) %collective-permute-start.2) | collective-permute-done | bytes 139296 | tf_op jit(solution)/shard_map/ppermute | solution.py:398
  10.8 2.0 %collective-permute-done.1 = bf16[272,256]{1,0:T(8,128)(2,1)S(1)} collective-permute-done((bf16[272,256]{1,0:T(8,128)(2,1)}, bf16[272,256]{1,0:T(8,128)(2,1)S(1)}, u32[]{:S(2)}, u32[]{:S(2)}) %collective-permute-start.1) | collective-permute-done | bytes 139296 | tf_op jit(solution)/shard_map/ppermute | solution.py:398
  14.3 1.8 %pad_maximum_fusion.gate_ref.refs_0_ = bf16[4,272,256]{2,1,0:T(8,128)(2,1)} fusion(bf16[1,272,256]{2,1,0:T(8,128)(2,1)S(1)} %bitcast.25, bf16[1,272,256]{2,1,0:T(8,128)(2,1)S(1)} %bitcast.26, bf16[1,272,256]{2,1,0:T(8,128)(2,1)S(1)} %bitcast.27, bf16[1,272,256]{2,1,0:T(8,128)(2,1)} %bitcast.24), kind=kLoop, calls=%fused_computation | loop fusion | flops 835584 | bytes 1114112 | tf_op jit(solution)/shard_map/stack | solution.py:426
  16.1 2.3 %prepare_queries.1 = (bf16[5,256,256]{2,1,0:T(8,128)(2,1)}, s32[1]{0:T(128)}) custom-call(f32[20]{0:T(128)} %reshape.9.bias_ref, bf16[256,640]{1,0:T(8,128)(2,1)} %query_ref.1, s32[1,256]{1,0:T(1,128)} %bitcast.29, bf16[4,272,256]{2,1,0:T(8,128)(2,1)} %pad_maximum_fusion.gate_ref.refs_0_), custom_call_target="tpu_custom_call" | custom-call | tf_op jit(solution)/shard_map/prepare_queries/pallas_call | solution.py:427
  18.8 2.0 %collective-permute-start.8 = (bf16[4,272,256]{2,1,0:T(8,128)(2,1)}, bf16[4,272,256]{2,1,0:T(8,128)(2,1)S(1)}, u32[]{:S(2)}, u32[]{:S(2)}) collective-permute-start(bf16[4,272,256]{2,1,0:T(8,128)(2,1)} %pad_maximum_fusion.gate_ref.refs_0_), channel_id=1, source_target_pairs={{0,224},{32,0},{64,32},{96,64},{128,96},{160,128},{192,160},{224,1... | collective-permute-start | bytes 1671176 | tf_op jit(solution)/shard_map/ppermute | solution.py:398
  22.1 2.4 %constant_dynamic-slice_fusion = (bf16[640,640]{1,0:T(8,128)(2,1)S(1)}, bf16[640,640]{1,0:T(8,128)(2,1)S(1)}) fusion(bf16[640,5120]{1,0:T(8,128)(2,1)} %weight_ref.1, s32[]{:T(128)S(6)} %select_n.78, s32[]{:T(128)S(6)} %select_n.76), kind=kLoop, calls=%fused_computation.6 | loop fusion | bytes 3276808 | tf_op jit(solution)/shard_map/dynamic_slice | solution.py:456
  24.5 1.7 %collective-permute-start.17 = (bf16[640,640]{1,0:T(8,128)(2,1)S(1)}, bf16[640,640]{1,0:T(8,128)(2,1)S(1)}, u32[]{:S(2)}, u32[]{:S(2)}) collective-permute-start(bf16[640,640]{1,0:T(8,128)(2,1)S(1)} %get-tuple-element.36), channel_id=1, source_target_pairs={{0,1},{1,2},{2,3},{3,0},{4,5},{5,6},{6,7},{7,4},{8,9},{9,10},{10,1... | collective-permute-start | bytes 2457608 | tf_op jit(solution)/shard_map/ppermute | solution.py:398
  26.2 1.7 %collective-permute-start.19 = (bf16[640,640]{1,0:T(8,128)(2,1)S(1)}, bf16[640,640]{1,0:T(8,128)(2,1)S(1)}, u32[]{:S(2)}, u32[]{:S(2)}) collective-permute-start(bf16[640,640]{1,0:T(8,128)(2,1)S(1)} %get-tuple-element.35), channel_id=1, source_target_pairs={{0,3},{1,0},{2,1},{3,2},{4,7},{5,4},{6,5},{7,6},{8,11},{9,8},{10,9... | collective-permute-start | bytes 2457608 | tf_op jit(solution)/shard_map/ppermute | solution.py:398
  27.8 7.0 %own_plane.1 = (f32[144,2560]{1,0:T(8,128)S(1)}, s32[1]{0:T(128)}) custom-call(s32[6]{0:T(128)S(1)} %stack.64.where_ref, bf16[5,256,256]{2,1,0:T(8,128)(2,1)S(1)} %copy-done.1, bf16[5,256,256]{2,1,0:T(8,128)(2,1)S(1)} %collective-permute-done.3.other_ref, bf16[4,272,256]{2,1,0:T(8,128)(2,1)S(1)} %copy-done), custom_call_target="tpu_custom_call" | custom-call | flops 5368709120 | bytes 1048576 | tf_op jit(solution)/shard_map/own_plane/pallas_call | solution.py:275
  38.6 2.1 %collective-permute-start.23 = (bf16[640,640]{1,0:T(8,128)(2,1)S(1)}, bf16[640,640]{1,0:T(8,128)(2,1)S(1)}, u32[]{:S(2)}, u32[]{:S(2)}) collective-permute-start(bf16[640,640]{1,0:T(8,128)(2,1)S(1)} %carve.1), channel_id=1, source_target_pairs={{0,2},{1,3},{2,0},{3,1},{4,6},{5,7},{6,4},{7,5},{8,10},{9,11},{10,... | collective-permute-start | bytes 2457608 | tf_op jit(solution)/shard_map/ppermute | solution.py:398
  40.6 7.4 %planes.3 = (f32[144,2560]{1,0:T(8,128)S(1)}, s32[1]{0:T(128)}) custom-call(s32[1]{0:T(128)} %bitcast.16.count_ref, bf16[5,256,256]{2,1,0:T(8,128)(2,1)S(1)} %copy-done.1, bf16[5,256,256]{2,1,0:T(8,128)(2,1)S(1)} %collective-permute-done.3.other_ref, bf16[4,272,256]{2,1,0:T(8,128)(2,1)S(1)} %collective-permute-done.4.refs_0_, ...), custom_call_target="tpu_custom_call" | custom-call | flops 8053063680 | bytes 1048576 | tf_op jit(solution)/shard_map/planes/pallas_call | solution.py:311
  49.5 2.8 %collective-permute-start.6 = (bf16[4,272,256]{2,1,0:T(8,128)(2,1)S(1)}, bf16[4,272,256]{2,1,0:T(8,128)(2,1)S(1)}, u32[]{:S(2)}, u32[]{:S(2)}) collective-permute-start(bf16[4,272,256]{2,1,0:T(8,128)(2,1)S(1)} %collective-permute-done.5.refs_0_), channel_id=1, source_target_pairs={{0,32},{32,64},{64,96},{96,128},{128,160},{160,192},{192,224},{224... | collective-permute-start | bytes 1671176 | tf_op jit(solution)/shard_map/ppermute | solution.py:398
  52.3 7.2 %planes.4 = (f32[144,2560]{1,0:T(8,128)S(1)}, s32[1]{0:T(128)}) custom-call(s32[1]{0:T(128)} %bitcast.15.count_ref, bf16[5,256,256]{2,1,0:T(8,128)(2,1)S(1)} %copy-done.1, bf16[5,256,256]{2,1,0:T(8,128)(2,1)S(1)} %collective-permute-done.3.other_ref, bf16[4,272,256]{2,1,0:T(8,128)(2,1)S(1)} %collective-permute-done.5.refs_0_, ...), custom_call_target="tpu_custom_call" | custom-call | flops 8053063680 | bytes 1048576 | tf_op jit(solution)/shard_map/planes/pallas_call | solution.py:311
  60.2 2.9 %collective-permute-start.7 = (bf16[2,272,256]{2,1,0:T(8,128)(2,1)S(1)}, bf16[2,272,256]{2,1,0:T(8,128)(2,1)S(1)}, u32[]{:S(2)}, u32[]{:S(2)}) collective-permute-start(bf16[2,272,256]{2,1,0:T(8,128)(2,1)S(1)} %slice.8.refs_3_), channel_id=1, source_target_pairs={{0,32},{32,64},{64,96},{96,128},{128,160},{160,192},{192,224},{224... | collective-permute-start | bytes 835592 | tf_op jit(solution)/shard_map/ppermute | solution.py:398
  63.3 7.4 %planes.5 = (f32[144,2560]{1,0:T(8,128)S(1)}, s32[1]{0:T(128)}) custom-call(s32[1]{0:T(128)} %bitcast.14.count_ref, bf16[5,256,256]{2,1,0:T(8,128)(2,1)S(1)} %copy-done.1, bf16[5,256,256]{2,1,0:T(8,128)(2,1)S(1)} %collective-permute-done.3.other_ref, bf16[4,272,256]{2,1,0:T(8,128)(2,1)S(1)} %collective-permute-done.6.refs_0_, ...), custom_call_target="tpu_custom_call" | custom-call | flops 8053063680 | bytes 1048576 | tf_op jit(solution)/shard_map/planes/pallas_call | solution.py:311
  71.0 4.7 %last_planes.1 = (f32[5,136,256]{2,1,0:T(8,128)S(1)}, bf16[5,144,256]{2,1,0:T(8,128)(2,1)S(1)}, s32[1]{0:T(128)}) custom-call(s32[1]{0:T(128)} %bitcast.1.count_ref, bf16[5,256,256]{2,1,0:T(8,128)(2,1)S(1)} %copy-done.1, bf16[5,256,256]{2,1,0:T(8,128)(2,1)S(1)} %collective-permute-done.3.other_ref, bf16[2,272,256]{2,1,0:T(8,128)(2,1)S(1)} %collective-permute-done.7.refs_0_, ...), custom_call_target="tpu_custom_call" | custom-call | flops 4026531840 | bytes 1048576 | tf_op jit(solution)/shard_map/last_planes/pallas_call | solution.py:311
  75.7 30.7 %collective-permute-start.12 = (bf16[5,144,256]{2,1,0:T(8,128)(2,1)S(1)}, bf16[5,144,256]{2,1,0:T(8,128)(2,1)S(1)}, u32[]{:S(2)}, u32[]{:S(2)}) collective-permute-start(bf16[5,144,256]{2,1,0:T(8,128)(2,1)S(1)} %get-tuple-element.28), channel_id=1, source_target_pairs={{0,4},{4,0},{1,5},{5,1},{2,6},{6,2},{3,7},{7,3},{8,12},{12,8},{9,1... | collective-permute-start | bytes 1105928 | tf_op jit(solution)/shard_map/ppermute | solution.py:398
  110.5 2.5 %collective-permute-start.16 = (bf16[128,640]{1,0:T(8,128)(2,1)}, bf16[128,640]{1,0:T(8,128)(2,1)}, u32[]{:S(2)}, u32[]{:S(2)}) collective-permute-start(bf16[128,640]{1,0:T(8,128)(2,1)} %get-tuple-element.30.own_1_), channel_id=1, source_target_pairs={{0,3},{1,0},{2,1},{3,2},{4,7},{5,4},{6,5},{7,6},{8,11},{9,8},{10,9... | collective-permute-start | bytes 491528 | tf_op jit(solution)/shard_map/ppermute | solution.py:398
  113.8 3.2 %collective-permute-start.15 = (bf16[128,640]{1,0:T(8,128)(2,1)S(1)}, bf16[128,640]{1,0:T(8,128)(2,1)S(1)}, u32[]{:S(2)}, u32[]{:S(2)}) collective-permute-start(bf16[128,640]{1,0:T(8,128)(2,1)S(1)} %get-tuple-element.29.own_0_), channel_id=1, source_target_pairs={{0,3},{1,0},{2,1},{3,2},{4,7},{5,4},{6,5},{7,6},{8,11},{9,8},{10,9... | collective-permute-start | bytes 491528 | tf_op jit(solution)/shard_map/ppermute | solution.py:398
  117.4 3.4 %collective-permute-start.22 = (bf16[128,640]{1,0:T(8,128)(2,1)}, bf16[128,640]{1,0:T(8,128)(2,1)S(1)}, u32[]{:S(2)}, u32[]{:S(2)}) collective-permute-start(bf16[128,640]{1,0:T(8,128)(2,1)} %collective-permute-done.16.above_1_), channel_id=1, source_target_pairs={{0,3},{1,0},{2,1},{3,2},{4,7},{5,4},{6,5},{7,6},{8,11},{9,8},{10,9... | collective-permute-start | bytes 491528 | tf_op jit(solution)/shard_map/ppermute | solution.py:398
  120.8 2.2 %constant_dynamic-slice_fusion.2.own_w = bf16[640,1280]{1,0:T(8,128)(2,1)S(1)} fusion(bf16[640,5120]{1,0:T(8,128)(2,1)} %weight_ref.1, s32[]{:T(128)S(6)} %select_n.74), kind=kLoop, calls=%fused_computation.8 | loop fusion | bytes 3276804 | tf_op jit(solution)/shard_map/dynamic_slice | solution.py:509
  123.0 3.3 %project_near.1.near_ref = f32[256,1280]{1,0:T(8,128)S(1)} custom-call(s32[1]{0:T(128)} %bitcast.core_ref, bf16[128,640]{1,0:T(8,128)(2,1)S(1)} %get-tuple-element.29.own_0_, bf16[128,640]{1,0:T(8,128)(2,1)} %get-tuple-element.30.own_1_, bf16[128,640]{1,0:T(8,128)(2,1)} %collective-permute-done.13.below_0_, ...), custom_call_target="tpu_custom_call" | custom-call | tf_op jit(solution)/shard_map/project_near/pallas_call | solution.py:355
  126.4 2.8 %project_far.1 = bf16[256,1280]{1,0:T(8,128)(2,1)} custom-call(s32[1]{0:T(128)} %bitcast.core_ref, f32[256,1280]{1,0:T(8,128)S(1)} %project_near.1.near_ref, bf16[128,640]{1,0:T(8,128)(2,1)S(1)} %collective-permute-done.21.pair_0_, bf16[128,640]{1,0:T(8,128)(2,1)S(1)} %collective-permute-done.22.pair_1_, bf16[640,640]{1,0:T(8,128)(2,1)S(1)} %broadcast_add_fusion.far_w_0_, ...), custom_call_target="tpu_custom_call" | custom-call | tf_op jit(solution)/shard_map/project_far/pallas_call | solution.py:367
  (59 shorter events, 14.6 us)
Async XLA Ops:
  1.7 9.1 %collective-permute-start.2 = (bf16[272,256]{1,0:T(8,128)(2,1)}, bf16[272,256]{1,0:T(8,128)(2,1)S(1)}, u32[]{:S(2)}, u32[]{:S(2)}) collective-permute-start(bf16[272,256]{1,0:T(8,128)(2,1)} %get-tuple-element.20), channel_id=1, source_target_pairs={{0,24},{8,0},{16,8},{24,16},{1,25},{9,1},{17,9},{25,17},{2,26},{10... | collective-permute-start | bytes 417800 | tf_op jit(solution)/shard_map/ppermute | solution.py:398
  4.5 8.3 %collective-permute-start.1 = (bf16[272,256]{1,0:T(8,128)(2,1)}, bf16[272,256]{1,0:T(8,128)(2,1)S(1)}, u32[]{:S(2)}, u32[]{:S(2)}) collective-permute-start(bf16[272,256]{1,0:T(8,128)(2,1)} %get-tuple-element.20), channel_id=1, source_target_pairs={{0,16},{8,24},{16,0},{24,8},{1,17},{9,25},{17,1},{25,9},{2,18},{10... | collective-permute-start | bytes 417800 | tf_op jit(solution)/shard_map/ppermute | solution.py:398
  5.3 9.0 %collective-permute-start = (bf16[272,256]{1,0:T(8,128)(2,1)}, bf16[272,256]{1,0:T(8,128)(2,1)S(1)}, u32[]{:S(2)}, u32[]{:S(2)}) collective-permute-start(bf16[272,256]{1,0:T(8,128)(2,1)} %get-tuple-element.20), channel_id=1, source_target_pairs={{0,8},{8,16},{16,24},{24,0},{1,9},{9,17},{17,25},{25,1},{2,10},{10... | collective-permute-start | bytes 417800 | tf_op jit(solution)/shard_map/ppermute | solution.py:398
  18.4 9.4 %collective-permute-start.3 = (bf16[5,256,256]{2,1,0:T(8,128)(2,1)}, bf16[5,256,256]{2,1,0:T(8,128)(2,1)S(1)}, u32[]{:S(2)}, u32[]{:S(2)}) collective-permute-start(bf16[5,256,256]{2,1,0:T(8,128)(2,1)} %get-tuple-element.21.mine_ref), channel_id=1, source_target_pairs={{0,4},{4,0},{1,5},{5,1},{2,6},{6,2},{3,7},{7,3},{8,12},{12,8},{9,1... | collective-permute-start | bytes 1966088 | tf_op jit(solution)/shard_map/ppermute | solution.py:398
  18.8 16.7 %collective-permute-start.4 = (bf16[4,272,256]{2,1,0:T(8,128)(2,1)}, bf16[4,272,256]{2,1,0:T(8,128)(2,1)S(1)}, u32[]{:S(2)}, u32[]{:S(2)}) collective-permute-start(bf16[4,272,256]{2,1,0:T(8,128)(2,1)} %pad_maximum_fusion.gate_ref.refs_0_), channel_id=1, source_target_pairs={{0,32},{32,64},{64,96},{96,128},{128,160},{160,192},{192,224},{224... | collective-permute-start | bytes 1671176 | tf_op jit(solution)/shard_map/ppermute | solution.py:398
  18.8 18.1 %collective-permute-start.8 = (bf16[4,272,256]{2,1,0:T(8,128)(2,1)}, bf16[4,272,256]{2,1,0:T(8,128)(2,1)S(1)}, u32[]{:S(2)}, u32[]{:S(2)}) collective-permute-start(bf16[4,272,256]{2,1,0:T(8,128)(2,1)} %pad_maximum_fusion.gate_ref.refs_0_), channel_id=1, source_target_pairs={{0,224},{32,0},{64,32},{96,64},{128,96},{160,128},{192,160},{224,1... | collective-permute-start | bytes 1671176 | tf_op jit(solution)/shard_map/ppermute | solution.py:398
  24.5 81.9 %collective-permute-start.17 = (bf16[640,640]{1,0:T(8,128)(2,1)S(1)}, bf16[640,640]{1,0:T(8,128)(2,1)S(1)}, u32[]{:S(2)}, u32[]{:S(2)}) collective-permute-start(bf16[640,640]{1,0:T(8,128)(2,1)S(1)} %get-tuple-element.36), channel_id=1, source_target_pairs={{0,1},{1,2},{2,3},{3,0},{4,5},{5,6},{6,7},{7,4},{8,9},{9,10},{10,1... | collective-permute-start | bytes 2457608 | tf_op jit(solution)/shard_map/ppermute | solution.py:398
  26.2 80.5 %collective-permute-start.19 = (bf16[640,640]{1,0:T(8,128)(2,1)S(1)}, bf16[640,640]{1,0:T(8,128)(2,1)S(1)}, u32[]{:S(2)}, u32[]{:S(2)}) collective-permute-start(bf16[640,640]{1,0:T(8,128)(2,1)S(1)} %get-tuple-element.35), channel_id=1, source_target_pairs={{0,3},{1,0},{2,1},{3,2},{4,7},{5,4},{6,5},{7,6},{8,11},{9,8},{10,9... | collective-permute-start | bytes 2457608 | tf_op jit(solution)/shard_map/ppermute | solution.py:398
  35.5 14.0 %collective-permute-start.5 = (bf16[4,272,256]{2,1,0:T(8,128)(2,1)S(1)}, bf16[4,272,256]{2,1,0:T(8,128)(2,1)S(1)}, u32[]{:S(2)}, u32[]{:S(2)}) collective-permute-start(bf16[4,272,256]{2,1,0:T(8,128)(2,1)S(1)} %broadcast_add_fusion.4), channel_id=1, source_target_pairs={{0,32},{32,64},{64,96},{96,128},{128,160},{160,192},{192,224},{224... | collective-permute-start | bytes 1671176 | tf_op jit(solution)/shard_map/ppermute | solution.py:398
  36.9 15.4 %collective-permute-start.9 = (bf16[4,272,256]{2,1,0:T(8,128)(2,1)S(1)}, bf16[4,272,256]{2,1,0:T(8,128)(2,1)S(1)}, u32[]{:S(2)}, u32[]{:S(2)}) collective-permute-start(bf16[4,272,256]{2,1,0:T(8,128)(2,1)S(1)} %broadcast_add_fusion.3), channel_id=1, source_target_pairs={{0,224},{32,0},{64,32},{96,64},{128,96},{160,128},{192,160},{224,1... | collective-permute-start | bytes 1671176 | tf_op jit(solution)/shard_map/ppermute | solution.py:398
  38.6 70.7 %collective-permute-start.23 = (bf16[640,640]{1,0:T(8,128)(2,1)S(1)}, bf16[640,640]{1,0:T(8,128)(2,1)S(1)}, u32[]{:S(2)}, u32[]{:S(2)}) collective-permute-start(bf16[640,640]{1,0:T(8,128)(2,1)S(1)} %carve.1), channel_id=1, source_target_pairs={{0,2},{1,3},{2,0},{3,1},{4,6},{5,7},{6,4},{7,5},{8,10},{9,11},{10,... | collective-permute-start | bytes 2457608 | tf_op jit(solution)/shard_map/ppermute | solution.py:398
  49.5 10.7 %collective-permute-start.6 = (bf16[4,272,256]{2,1,0:T(8,128)(2,1)S(1)}, bf16[4,272,256]{2,1,0:T(8,128)(2,1)S(1)}, u32[]{:S(2)}, u32[]{:S(2)}) collective-permute-start(bf16[4,272,256]{2,1,0:T(8,128)(2,1)S(1)} %collective-permute-done.5.refs_0_), channel_id=1, source_target_pairs={{0,32},{32,64},{64,96},{96,128},{128,160},{160,192},{192,224},{224... | collective-permute-start | bytes 1671176 | tf_op jit(solution)/shard_map/ppermute | solution.py:398
  52.3 10.8 %collective-permute-start.10 = (bf16[4,272,256]{2,1,0:T(8,128)(2,1)S(1)}, bf16[4,272,256]{2,1,0:T(8,128)(2,1)S(1)}, u32[]{:S(2)}, u32[]{:S(2)}) collective-permute-start(bf16[4,272,256]{2,1,0:T(8,128)(2,1)S(1)} %collective-permute-done.9.refs_1_), channel_id=1, source_target_pairs={{0,224},{32,0},{64,32},{96,64},{128,96},{160,128},{192,160},{224,1... | collective-permute-start | bytes 1671176 | tf_op jit(solution)/shard_map/ppermute | solution.py:398
  60.2 10.5 %collective-permute-start.7 = (bf16[2,272,256]{2,1,0:T(8,128)(2,1)S(1)}, bf16[2,272,256]{2,1,0:T(8,128)(2,1)S(1)}, u32[]{:S(2)}, u32[]{:S(2)}) collective-permute-start(bf16[2,272,256]{2,1,0:T(8,128)(2,1)S(1)} %slice.8.refs_3_), channel_id=1, source_target_pairs={{0,32},{32,64},{64,96},{96,128},{128,160},{160,192},{192,224},{224... | collective-permute-start | bytes 835592 | tf_op jit(solution)/shard_map/ppermute | solution.py:398
  63.2 7.8 %collective-permute-start.11 = (bf16[2,272,256]{2,1,0:T(8,128)(2,1)S(1)}, bf16[2,272,256]{2,1,0:T(8,128)(2,1)S(1)}, u32[]{:S(2)}, u32[]{:S(2)}) collective-permute-start(bf16[2,272,256]{2,1,0:T(8,128)(2,1)S(1)} %slice.9.refs_4_), channel_id=1, source_target_pairs={{0,224},{32,0},{64,32},{96,64},{128,96},{160,128},{192,160},{224,1... | collective-permute-start | bytes 835592 | tf_op jit(solution)/shard_map/ppermute | solution.py:398
  75.7 32.1 %collective-permute-start.12 = (bf16[5,144,256]{2,1,0:T(8,128)(2,1)S(1)}, bf16[5,144,256]{2,1,0:T(8,128)(2,1)S(1)}, u32[]{:S(2)}, u32[]{:S(2)}) collective-permute-start(bf16[5,144,256]{2,1,0:T(8,128)(2,1)S(1)} %get-tuple-element.28), channel_id=1, source_target_pairs={{0,4},{4,0},{1,5},{5,1},{2,6},{6,2},{3,7},{7,3},{8,12},{12,8},{9,1... | collective-permute-start | bytes 1105928 | tf_op jit(solution)/shard_map/ppermute | solution.py:398
  106.5 7.2 %collective-permute-start.18 = (bf16[640,640]{1,0:T(8,128)(2,1)S(1)}, bf16[640,640]{1,0:T(8,128)(2,1)S(1)}, u32[]{:S(2)}, u32[]{:S(2)}) collective-permute-start(bf16[640,640]{1,0:T(8,128)(2,1)S(1)} %broadcast_add_fusion.2.up_w_0_), channel_id=1, source_target_pairs={{0,4},{4,0},{1,5},{5,1},{2,6},{6,2},{3,7},{7,3},{8,12},{12,8},{9,1... | collective-permute-start | bytes 2457608 | tf_op jit(solution)/shard_map/ppermute | solution.py:398
  106.7 7.1 %collective-permute-start.20 = (bf16[640,640]{1,0:T(8,128)(2,1)S(1)}, bf16[640,640]{1,0:T(8,128)(2,1)}, u32[]{:S(2)}, u32[]{:S(2)}) collective-permute-start(bf16[640,640]{1,0:T(8,128)(2,1)S(1)} %broadcast_add_fusion.1.down_w_0_), channel_id=1, source_target_pairs={{0,4},{4,0},{1,5},{5,1},{2,6},{6,2},{3,7},{7,3},{8,12},{12,8},{9,1... | collective-permute-start | bytes 2457608 | tf_op jit(solution)/shard_map/ppermute | solution.py:398
  109.4 17.0 %collective-permute-start.24 = (bf16[640,640]{1,0:T(8,128)(2,1)S(1)}, bf16[640,640]{1,0:T(8,128)(2,1)}, u32[]{:S(2)}, u32[]{:S(2)}) collective-permute-start(bf16[640,640]{1,0:T(8,128)(2,1)S(1)} %broadcast_add_fusion.far_w_0_), channel_id=1, source_target_pairs={{0,4},{4,0},{1,5},{5,1},{2,6},{6,2},{3,7},{7,3},{8,12},{12,8},{9,1... | collective-permute-start | bytes 2457608 | tf_op jit(solution)/shard_map/ppermute | solution.py:398
  109.8 7.6 %collective-permute-start.13 = (bf16[128,640]{1,0:T(8,128)(2,1)S(1)}, bf16[128,640]{1,0:T(8,128)(2,1)}, u32[]{:S(2)}, u32[]{:S(2)}) collective-permute-start(bf16[128,640]{1,0:T(8,128)(2,1)S(1)} %get-tuple-element.29.own_0_), channel_id=1, source_target_pairs={{0,1},{1,2},{2,3},{3,0},{4,5},{5,6},{6,7},{7,4},{8,9},{9,10},{10,1... | collective-permute-start | bytes 491528 | tf_op jit(solution)/shard_map/ppermute | solution.py:398
  113.7 9.3 %collective-permute-start.14 = (bf16[128,640]{1,0:T(8,128)(2,1)}, bf16[128,640]{1,0:T(8,128)(2,1)S(1)}, u32[]{:S(2)}, u32[]{:S(2)}) collective-permute-start(bf16[128,640]{1,0:T(8,128)(2,1)} %get-tuple-element.30.own_1_), channel_id=1, source_target_pairs={{0,1},{1,2},{2,3},{3,0},{4,5},{5,6},{6,7},{7,4},{8,9},{9,10},{10,1... | collective-permute-start | bytes 491528 | tf_op jit(solution)/shard_map/ppermute | solution.py:398
  113.8 9.2 %collective-permute-start.15 = (bf16[128,640]{1,0:T(8,128)(2,1)S(1)}, bf16[128,640]{1,0:T(8,128)(2,1)S(1)}, u32[]{:S(2)}, u32[]{:S(2)}) collective-permute-start(bf16[128,640]{1,0:T(8,128)(2,1)S(1)} %get-tuple-element.29.own_0_), channel_id=1, source_target_pairs={{0,3},{1,0},{2,1},{3,2},{4,7},{5,4},{6,5},{7,6},{8,11},{9,8},{10,9... | collective-permute-start | bytes 491528 | tf_op jit(solution)/shard_map/ppermute | solution.py:398
  117.4 8.9 %collective-permute-start.21 = (bf16[128,640]{1,0:T(8,128)(2,1)}, bf16[128,640]{1,0:T(8,128)(2,1)S(1)}, u32[]{:S(2)}, u32[]{:S(2)}) collective-permute-start(bf16[128,640]{1,0:T(8,128)(2,1)} %collective-permute-done.13.below_0_), channel_id=1, source_target_pairs={{0,1},{1,2},{2,3},{3,0},{4,5},{5,6},{6,7},{7,4},{8,9},{9,10},{10,1... | collective-permute-start | bytes 491528 | tf_op jit(solution)/shard_map/ppermute | solution.py:398
  117.4 8.9 %collective-permute-start.22 = (bf16[128,640]{1,0:T(8,128)(2,1)}, bf16[128,640]{1,0:T(8,128)(2,1)S(1)}, u32[]{:S(2)}, u32[]{:S(2)}) collective-permute-start(bf16[128,640]{1,0:T(8,128)(2,1)} %collective-permute-done.16.above_1_), channel_id=1, source_target_pairs={{0,3},{1,0},{2,1},{3,2},{4,7},{5,4},{6,5},{7,6},{8,11},{9,8},{10,9... | collective-permute-start | bytes 491528 | tf_op jit(solution)/shard_map/ppermute | solution.py:398
  (5 other events, 42.8 us)
where the time goes:
time: 129 us
  starting transfers between devices  61.8 us (48%)
  Pallas kernels  44.8 us (35%)
  waiting for transfers between devices  9.32 us (7%)
  local copies, waits for them, and re-layouts  6.14 us (5%)
  between operations  4.97 us (4%)
  other arithmetic  2.1 us (2%)
    ppermute x25, starting transfers between devices, shift(): lax.ppermute(value, axis, [(i, (i + step) % size) for i in range(size)])  61.8 us
    pallas_call x4, Pallas kernels, attend_planes(): pl.pallas_call(functools.partial(plane_kernel, plan, last, len(gates)), i...  26.8 us
    ppermute x25, waiting for transfers between devices, shift(): lax.ppermute(value, axis, [(i, (i + step) % size) for i in range(size)])  9.32 us
    pallas_call x1, Pallas kernels, attend_own(): pl.pallas_call(functools.partial(own_kernel, len(msgs)), in_specs=[IN_SME...  6.98 us
    pallas_call x1, Pallas kernels, project_near(): pl.pallas_call(near_kernel, in_specs=[IN_SMEM, pair, pair, pair, IN_VMEM,...  3.28 us
    pallas_call x1, Pallas kernels, project_far(): pl.pallas_call(far_kernel, in_specs=[IN_SMEM, IN_VMEM, pair, pair], out_s...  2.75 us
  transfers between devices with their start and end apart: 25, of which 7 were waited for; matrix products, arithmetic and copies ran while one was open for 5% of the time, Pallas kernels for 29%

commit v1 on v0

--- a/solution.py
+++ b/solution.py
@@ -438,10 +438,17 @@
 
     forward, backward = [plane], [plane]
 
+    def up(step):
+        return [(i, i + 1) for i in range(step - 1, nz - 1)]
+
+    def down(step):
+        return [((q - step + 1) % nz, (q - step) % nz) for q in range(nz // 2)]
+
     def onward(token):
         zero = 0 if token is None else token[0].astype(bf16)
-        forward.append(shift(forward[-1] + zero, "z", nz, 1))
-        backward.append(shift(backward[-1] + zero, "z", nz, -1))
+        step = len(forward)
+        forward.append(lax.ppermute(forward[-1] + zero, "z", up(step)))
+        backward.append(lax.ppermute(backward[-1] + zero, "z", down(step)))
 
     onward(None)
 
@@ -471,7 +478,10 @@
     onward(token)
     onward(None)
     far_parts = [forward[3][: nx // 2], backward[3][nx // 2 :]]
-    far = [shift(far_parts[0], "z", nz, 1), shift(far_parts[1], "z", nz, -1)]
+    far = [
+        lax.ppermute(far_parts[0], "z", up(nz // 2)),
+        lax.ppermute(far_parts[1], "z", down(nz // 2)),
+    ]
     planes = tuple(tuple((i, j) for j in range(nx)) for i in range(2))
     for step in (1, 2, 3):
         count = jnp.stack([jnp.where(zi >= nz - step, 2, jnp.where(zi >= step, 1, 0))])

time: 129 us -> 142 us (1.10)
  starting transfers between devices: 61.8 us -> 74.5 us
    ppermute x0 -> x8, starting transfers between devices: none -> 18.2 us  [the longest x3 8.46 us: onward(): backward.append(lax.ppermute(backward[-1] + zero, 'z', down(step)))]
    ppermute x25 -> x17, starting transfers between devices: 61.8 us -> 56.3 us  [shift(): lax.ppermute(value, axis, [(i, (i + step) % size) for i in range(size)])]
    ppermute x0 -> x8, waiting for transfers between devices: none -> 2.01 us  [the longest x3 1.99 us: onward(): backward.append(lax.ppermute(backward[-1] + zero, 'z', down(step)))]
    ppermute x25 -> x17, waiting for transfers between devices: 9.32 us -> 7.58 us  [shift(): lax.ppermute(value, axis, [(i, (i + step) % size) for i in range(size)])]
  transfers between devices with their start and end apart: 25 -> 25, of which waited for: 7 -> 7; matrix products, arithmetic and copies ran while one was open for 5% -> 5% of each run, Pallas kernels for 29% -> 27%
where the time goes in v1:
time: 142 us
  starting transfers between devices  74.5 us (52%)
  Pallas kernels  44.5 us (31%)
  waiting for transfers between devices  9.58 us (7%)
  local copies, waits for them, and re-layouts  6.14 us (4%)
  between operations  5.03 us (4%)
  other arithmetic  2.1 us (1%)
    ppermute x17, starting transfers between devices, shift(): lax.ppermute(value, axis, [(i, (i + step) % size) for i in range(size)])  56.3 us
    pallas_call x4, Pallas kernels, attend_planes(): pl.pallas_call(functools.partial(plane_kernel, plan, last, len(gates)), i...  26.5 us
    ppermute x3, starting transfers between devices, onward(): backward.append(lax.ppermute(backward[-1] + zero, 'z', down(step)))  8.46 us
    ppermute x17, waiting for transfers between devices, shift(): lax.ppermute(value, axis, [(i, (i + step) % size) for i in range(size)])  7.58 us
    pallas_call x1, Pallas kernels, attend_own(): pl.pallas_call(functools.partial(own_kernel, len(msgs)), in_specs=[IN_SME...  6.98 us
    ppermute x1, starting transfers between devices, shards(): lax.ppermute(far_parts[1], 'z', down(nz // 2))  4.55 us
    ppermute x3, starting transfers between devices, onward(): forward.append(lax.ppermute(forward[-1] + zero, 'z', up(step)))  3.87 us
    pallas_call x1, Pallas kernels, project_near(): pl.pallas_call(near_kernel, in_specs=[IN_SMEM, pair, pair, pair, IN_VMEM,...  3.28 us
  transfers between devices with their start and end apart: 25, of which 7 were waited for; matrix products, arithmetic and copies ran while one was open for 5% of the time, Pallas kernels for 27%

profile of v1, /device:TPU:224, one launch (start us, length us, event | category | flops | bytes accessed | tf_op | source)
XLA Modules:
  0.0 141.8 jit_solution(568459808076213820)
XLA Ops:
  1.7 2.8 %collective-permute-start.2 = (bf16[272,256]{1,0:T(8,128)(2,1)}, bf16[272,256]{1,0:T(8,128)(2,1)S(1)}, u32[]{:S(2)}, u32[]{:S(2)}) collective-permute-start(bf16[272,256]{1,0:T(8,128)(2,1)} %get-tuple-element.20), channel_id=1, source_target_pairs={{0,24},{8,0},{16,8},{24,16},{1,25},{9,1},{17,9},{25,17},{2,26},{10... | collective-permute-start | bytes 417800 | tf_op jit(solution)/shard_map/ppermute | solution.py:398
  7.6 3.2 %collective-permute-done.2 = bf16[272,256]{1,0:T(8,128)(2,1)S(1)} collective-permute-done((bf16[272,256]{1,0:T(8,128)(2,1)}, bf16[272,256]{1,0:T(8,128)(2,1)S(1)}, u32[]{:S(2)}, u32[]{:S(2)}) %collective-permute-start.2) | collective-permute-done | bytes 139296 | tf_op jit(solution)/shard_map/ppermute | solution.py:398
  10.8 2.0 %collective-permute-done.1 = bf16[272,256]{1,0:T(8,128)(2,1)S(1)} collective-permute-done((bf16[272,256]{1,0:T(8,128)(2,1)}, bf16[272,256]{1,0:T(8,128)(2,1)S(1)}, u32[]{:S(2)}, u32[]{:S(2)}) %collective-permute-start.1) | collective-permute-done | bytes 139296 | tf_op jit(solution)/shard_map/ppermute | solution.py:398
  14.3 1.8 %pad_maximum_fusion.gate_ref.refs_0_ = bf16[4,272,256]{2,1,0:T(8,128)(2,1)} fusion(bf16[1,272,256]{2,1,0:T(8,128)(2,1)S(1)} %bitcast.25, bf16[1,272,256]{2,1,0:T(8,128)(2,1)S(1)} %bitcast.26, bf16[1,272,256]{2,1,0:T(8,128)(2,1)S(1)} %bitcast.27, bf16[1,272,256]{2,1,0:T(8,128)(2,1)} %bitcast.24), kind=kLoop, calls=%fused_computation | loop fusion | flops 835584 | bytes 1114112 | tf_op jit(solution)/shard_map/stack | solution.py:426
  16.1 2.3 %prepare_queries.1 = (bf16[5,256,256]{2,1,0:T(8,128)(2,1)}, s32[1]{0:T(128)}) custom-call(f32[20]{0:T(128)} %reshape.9.bias_ref, bf16[256,640]{1,0:T(8,128)(2,1)} %query_ref.1, s32[1,256]{1,0:T(1,128)} %bitcast.29, bf16[4,272,256]{2,1,0:T(8,128)(2,1)} %pad_maximum_fusion.gate_ref.refs_0_), custom_call_target="tpu_custom_call" | custom-call | tf_op jit(solution)/shard_map/prepare_queries/pallas_call | solution.py:427
  22.6 2.4 %constant_dynamic-slice_fusion = (bf16[640,640]{1,0:T(8,128)(2,1)S(1)}, bf16[640,640]{1,0:T(8,128)(2,1)S(1)}) fusion(bf16[640,5120]{1,0:T(8,128)(2,1)} %weight_ref.1, s32[]{:T(128)S(6)} %select_n.78, s32[]{:T(128)S(6)} %select_n.76), kind=kLoop, calls=%fused_computation.6 | loop fusion | bytes 3276808 | tf_op jit(solution)/shard_map/dynamic_slice | solution.py:463
  25.0 1.7 %collective-permute-start.17 = (bf16[640,640]{1,0:T(8,128)(2,1)S(1)}, bf16[640,640]{1,0:T(8,128)(2,1)S(1)}, u32[]{:S(2)}, u32[]{:S(2)}) collective-permute-start(bf16[640,640]{1,0:T(8,128)(2,1)S(1)} %get-tuple-element.36), channel_id=1, source_target_pairs={{0,1},{1,2},{2,3},{3,0},{4,5},{5,6},{6,7},{7,4},{8,9},{9,10},{10,1... | collective-permute-start | bytes 2457608 | tf_op jit(solution)/shard_map/ppermute | solution.py:398
  26.7 1.7 %collective-permute-start.19 = (bf16[640,640]{1,0:T(8,128)(2,1)S(1)}, bf16[640,640]{1,0:T(8,128)(2,1)S(1)}, u32[]{:S(2)}, u32[]{:S(2)}) collective-permute-start(bf16[640,640]{1,0:T(8,128)(2,1)S(1)} %get-tuple-element.35), channel_id=1, source_target_pairs={{0,3},{1,0},{2,1},{3,2},{4,7},{5,4},{6,5},{7,6},{8,11},{9,8},{10,9... | collective-permute-start | bytes 2457608 | tf_op jit(solution)/shard_map/ppermute | solution.py:398
  28.4 7.0 %own_plane.1 = (f32[144,2560]{1,0:T(8,128)S(1)}, s32[1]{0:T(128)}) custom-call(s32[6]{0:T(128)S(1)} %stack.64.where_ref, bf16[5,256,256]{2,1,0:T(8,128)(2,1)S(1)} %copy-done.1, bf16[5,256,256]{2,1,0:T(8,128)(2,1)S(1)} %collective-permute-done.3.other_ref, bf16[4,272,256]{2,1,0:T(8,128)(2,1)S(1)} %copy-done), custom_call_target="tpu_custom_call" | custom-call | flops 5368709120 | bytes 1048576 | tf_op jit(solution)/shard_map/own_plane/pallas_call | solution.py:275
  38.3 3.7 %collective-permute-start.9 = (bf16[4,272,256]{2,1,0:T(8,128)(2,1)S(1)}, bf16[4,272,256]{2,1,0:T(8,128)(2,1)S(1)}, u32[]{:S(2)}, u32[]{:S(2)}) collective-permute-start(bf16[4,272,256]{2,1,0:T(8,128)(2,1)S(1)} %broadcast_add_fusion.3), channel_id=1, source_target_pairs={{224,192},{0,224},{32,0},{64,32},{225,193},{1,225},{33,1},{65,33},... | collective-permute-start | bytes 1671176 | tf_op jit(solution)/shard_map/ppermute | solution.py:451
  42.8 3.0 %collective-permute-start.23 = (bf16[640,640]{1,0:T(8,128)(2,1)S(1)}, bf16[640,640]{1,0:T(8,128)(2,1)S(1)}, u32[]{:S(2)}, u32[]{:S(2)}) collective-permute-start(bf16[640,640]{1,0:T(8,128)(2,1)S(1)} %carve.1), channel_id=1, source_target_pairs={{0,2},{1,3},{2,0},{3,1},{4,6},{5,7},{6,4},{7,5},{8,10},{9,11},{10,... | collective-permute-start | bytes 2457608 | tf_op jit(solution)/shard_map/ppermute | solution.py:398
  45.8 7.2 %planes.3 = (f32[144,2560]{1,0:T(8,128)S(1)}, s32[1]{0:T(128)}) custom-call(s32[1]{0:T(128)} %bitcast.16.count_ref, bf16[5,256,256]{2,1,0:T(8,128)(2,1)S(1)} %copy-done.1, bf16[5,256,256]{2,1,0:T(8,128)(2,1)S(1)} %collective-permute-done.3.other_ref, bf16[4,272,256]{2,1,0:T(8,128)(2,1)S(1)} %collective-permute-done.4.refs_0_, ...), custom_call_target="tpu_custom_call" | custom-call | flops 8053063680 | bytes 1048576 | tf_op jit(solution)/shard_map/planes/pallas_call | solution.py:311
  55.5 3.4 %collective-permute-start.10 = (bf16[4,272,256]{2,1,0:T(8,128)(2,1)S(1)}, bf16[4,272,256]{2,1,0:T(8,128)(2,1)S(1)}, u32[]{:S(2)}, u32[]{:S(2)}) collective-permute-start(bf16[4,272,256]{2,1,0:T(8,128)(2,1)S(1)} %collective-permute-done.9.refs_1_), channel_id=1, source_target_pairs={{192,160},{224,192},{0,224},{32,0},{193,161},{225,193},{1,225},{33... | collective-permute-start | bytes 1671176 | tf_op jit(solution)/shard_map/ppermute | solution.py:451
  58.9 7.4 %planes.4 = (f32[144,2560]{1,0:T(8,128)S(1)}, s32[1]{0:T(128)}) custom-call(s32[1]{0:T(128)} %bitcast.15.count_ref, bf16[5,256,256]{2,1,0:T(8,128)(2,1)S(1)} %copy-done.1, bf16[5,256,256]{2,1,0:T(8,128)(2,1)S(1)} %collective-permute-done.3.other_ref, bf16[4,272,256]{2,1,0:T(8,128)(2,1)S(1)} %collective-permute-done.5.refs_0_, ...), custom_call_target="tpu_custom_call" | custom-call | flops 8053063680 | bytes 1048576 | tf_op jit(solution)/shard_map/planes/pallas_call | solution.py:311
  68.3 4.6 %collective-permute-start.11 = (bf16[2,272,256]{2,1,0:T(8,128)(2,1)S(1)}, bf16[2,272,256]{2,1,0:T(8,128)(2,1)S(1)}, u32[]{:S(2)}, u32[]{:S(2)}) collective-permute-start(bf16[2,272,256]{2,1,0:T(8,128)(2,1)S(1)} %slice.9.refs_4_), channel_id=1, source_target_pairs={{160,128},{192,160},{224,192},{0,224},{161,129},{193,161},{225,193... | collective-permute-start | bytes 835592 | tf_op jit(solution)/shard_map/ppermute | solution.py:483
  72.9 7.2 %planes.5 = (f32[144,2560]{1,0:T(8,128)S(1)}, s32[1]{0:T(128)}) custom-call(s32[1]{0:T(128)} %bitcast.14.count_ref, bf16[5,256,256]{2,1,0:T(8,128)(2,1)S(1)} %copy-done.1, bf16[5,256,256]{2,1,0:T(8,128)(2,1)S(1)} %collective-permute-done.3.other_ref, bf16[4,272,256]{2,1,0:T(8,128)(2,1)S(1)} %collective-permute-done.6.refs_0_, ...), custom_call_target="tpu_custom_call" | custom-call | flops 8053063680 | bytes 1048576 | tf_op jit(solution)/shard_map/planes/pallas_call | solution.py:311
  80.2 4.7 %last_planes.1 = (f32[5,136,256]{2,1,0:T(8,128)S(1)}, bf16[5,144,256]{2,1,0:T(8,128)(2,1)S(1)}, s32[1]{0:T(128)}) custom-call(s32[1]{0:T(128)} %bitcast.1.count_ref, bf16[5,256,256]{2,1,0:T(8,128)(2,1)S(1)} %copy-done.1, bf16[5,256,256]{2,1,0:T(8,128)(2,1)S(1)} %collective-permute-done.3.other_ref, bf16[2,272,256]{2,1,0:T(8,128)(2,1)S(1)} %collective-permute-done.7.refs_0_, ...), custom_call_target="tpu_custom_call" | custom-call | flops 4026531840 | bytes 1048576 | tf_op jit(solution)/shard_map/last_planes/pallas_call | solution.py:311
  84.8 34.3 %collective-permute-start.12 = (bf16[5,144,256]{2,1,0:T(8,128)(2,1)S(1)}, bf16[5,144,256]{2,1,0:T(8,128)(2,1)S(1)}, u32[]{:S(2)}, u32[]{:S(2)}) collective-permute-start(bf16[5,144,256]{2,1,0:T(8,128)(2,1)S(1)} %get-tuple-element.28), channel_id=1, source_target_pairs={{0,4},{4,0},{1,5},{5,1},{2,6},{6,2},{3,7},{7,3},{8,12},{12,8},{9,1... | collective-permute-start | bytes 1105928 | tf_op jit(solution)/shard_map/ppermute | solution.py:398
  123.2 2.6 %collective-permute-start.16 = (bf16[128,640]{1,0:T(8,128)(2,1)}, bf16[128,640]{1,0:T(8,128)(2,1)}, u32[]{:S(2)}, u32[]{:S(2)}) collective-permute-start(bf16[128,640]{1,0:T(8,128)(2,1)} %get-tuple-element.30.own_1_), channel_id=1, source_target_pairs={{0,3},{1,0},{2,1},{3,2},{4,7},{5,4},{6,5},{7,6},{8,11},{9,8},{10,9... | collective-permute-start | bytes 491528 | tf_op jit(solution)/shard_map/ppermute | solution.py:398
  126.6 3.2 %collective-permute-start.15 = (bf16[128,640]{1,0:T(8,128)(2,1)S(1)}, bf16[128,640]{1,0:T(8,128)(2,1)S(1)}, u32[]{:S(2)}, u32[]{:S(2)}) collective-permute-start(bf16[128,640]{1,0:T(8,128)(2,1)S(1)} %get-tuple-element.29.own_0_), channel_id=1, source_target_pairs={{0,3},{1,0},{2,1},{3,2},{4,7},{5,4},{6,5},{7,6},{8,11},{9,8},{10,9... | collective-permute-start | bytes 491528 | tf_op jit(solution)/shard_map/ppermute | solution.py:398
  130.1 3.4 %collective-permute-start.22 = (bf16[128,640]{1,0:T(8,128)(2,1)}, bf16[128,640]{1,0:T(8,128)(2,1)S(1)}, u32[]{:S(2)}, u32[]{:S(2)}) collective-permute-start(bf16[128,640]{1,0:T(8,128)(2,1)} %collective-permute-done.16.above_1_), channel_id=1, source_target_pairs={{0,3},{1,0},{2,1},{3,2},{4,7},{5,4},{6,5},{7,6},{8,11},{9,8},{10,9... | collective-permute-start | bytes 491528 | tf_op jit(solution)/shard_map/ppermute | solution.py:398
  133.5 2.2 %constant_dynamic-slice_fusion.2.own_w = bf16[640,1280]{1,0:T(8,128)(2,1)S(1)} fusion(bf16[640,5120]{1,0:T(8,128)(2,1)} %weight_ref.1, s32[]{:T(128)S(6)} %select_n.74), kind=kLoop, calls=%fused_computation.8 | loop fusion | bytes 3276804 | tf_op jit(solution)/shard_map/dynamic_slice | solution.py:519
  135.8 3.3 %project_near.1.near_ref = f32[256,1280]{1,0:T(8,128)S(1)} custom-call(s32[1]{0:T(128)} %bitcast.core_ref, bf16[128,640]{1,0:T(8,128)(2,1)S(1)} %get-tuple-element.29.own_0_, bf16[128,640]{1,0:T(8,128)(2,1)} %get-tuple-element.30.own_1_, bf16[128,640]{1,0:T(8,128)(2,1)} %collective-permute-done.13.below_0_, ...), custom_call_target="tpu_custom_call" | custom-call | tf_op jit(solution)/shard_map/project_near/pallas_call | solution.py:355
  139.1 2.8 %project_far.1 = bf16[256,1280]{1,0:T(8,128)(2,1)} custom-call(s32[1]{0:T(128)} %bitcast.core_ref, f32[256,1280]{1,0:T(8,128)S(1)} %project_near.1.near_ref, bf16[128,640]{1,0:T(8,128)(2,1)S(1)} %collective-permute-done.21.pair_0_, bf16[128,640]{1,0:T(8,128)(2,1)S(1)} %collective-permute-done.22.pair_1_, bf16[640,640]{1,0:T(8,128)(2,1)S(1)} %broadcast_add_fusion.far_w_0_, ...), custom_call_target="tpu_custom_call" | custom-call | tf_op jit(solution)/shard_map/project_far/pallas_call | solution.py:367
  (59 shorter events, 19.0 us)
Async XLA Ops:
  1.7 9.1 %collective-permute-start.2 = (bf16[272,256]{1,0:T(8,128)(2,1)}, bf16[272,256]{1,0:T(8,128)(2,1)S(1)}, u32[]{:S(2)}, u32[]{:S(2)}) collective-permute-start(bf16[272,256]{1,0:T(8,128)(2,1)} %get-tuple-element.20), channel_id=1, source_target_pairs={{0,24},{8,0},{16,8},{24,16},{1,25},{9,1},{17,9},{25,17},{2,26},{10... | collective-permute-start | bytes 417800 | tf_op jit(solution)/shard_map/ppermute | solution.py:398
  4.5 8.3 %collective-permute-start.1 = (bf16[272,256]{1,0:T(8,128)(2,1)}, bf16[272,256]{1,0:T(8,128)(2,1)S(1)}, u32[]{:S(2)}, u32[]{:S(2)}) collective-permute-start(bf16[272,256]{1,0:T(8,128)(2,1)} %get-tuple-element.20), channel_id=1, source_target_pairs={{0,16},{8,24},{16,0},{24,8},{1,17},{9,25},{17,1},{25,9},{2,18},{10... | collective-permute-start | bytes 417800 | tf_op jit(solution)/shard_map/ppermute | solution.py:398
  5.3 9.0 %collective-permute-start = (bf16[272,256]{1,0:T(8,128)(2,1)}, bf16[272,256]{1,0:T(8,128)(2,1)S(1)}, u32[]{:S(2)}, u32[]{:S(2)}) collective-permute-start(bf16[272,256]{1,0:T(8,128)(2,1)} %get-tuple-element.20), channel_id=1, source_target_pairs={{0,8},{8,16},{16,24},{24,0},{1,9},{9,17},{17,25},{25,1},{2,10},{10... | collective-permute-start | bytes 417800 | tf_op jit(solution)/shard_map/ppermute | solution.py:398
  18.4 9.9 %collective-permute-start.3 = (bf16[5,256,256]{2,1,0:T(8,128)(2,1)}, bf16[5,256,256]{2,1,0:T(8,128)(2,1)S(1)}, u32[]{:S(2)}, u32[]{:S(2)}) collective-permute-start(bf16[5,256,256]{2,1,0:T(8,128)(2,1)} %get-tuple-element.21.mine_ref), channel_id=1, source_target_pairs={{0,4},{4,0},{1,5},{5,1},{2,6},{6,2},{3,7},{7,3},{8,12},{12,8},{9,1... | collective-permute-start | bytes 1966088 | tf_op jit(solution)/shard_map/ppermute | solution.py:398
  18.8 17.2 %collective-permute-start.4 = (bf16[4,272,256]{2,1,0:T(8,128)(2,1)}, bf16[4,272,256]{2,1,0:T(8,128)(2,1)S(1)}, u32[]{:S(2)}, u32[]{:S(2)}) collective-permute-start(bf16[4,272,256]{2,1,0:T(8,128)(2,1)} %pad_maximum_fusion.gate_ref.refs_0_), channel_id=1, source_target_pairs={{0,32},{32,64},{64,96},{96,128},{128,160},{160,192},{192,224},{1,3... | collective-permute-start | bytes 1671176 | tf_op jit(solution)/shard_map/ppermute | solution.py:450
  20.1 18.2 %collective-permute-start.8 = (bf16[4,272,256]{2,1,0:T(8,128)(2,1)}, bf16[4,272,256]{2,1,0:T(8,128)(2,1)S(1)}, u32[]{:S(2)}, u32[]{:S(2)}) collective-permute-start(bf16[4,272,256]{2,1,0:T(8,128)(2,1)} %pad_maximum_fusion.gate_ref.refs_0_), channel_id=1, source_target_pairs={{0,224},{32,0},{64,32},{96,64},{1,225},{33,1},{65,33},{97,65},{2,2... | collective-permute-start | bytes 1671176 | tf_op jit(solution)/shard_map/ppermute | solution.py:451
  25.0 94.1 %collective-permute-start.17 = (bf16[640,640]{1,0:T(8,128)(2,1)S(1)}, bf16[640,640]{1,0:T(8,128)(2,1)S(1)}, u32[]{:S(2)}, u32[]{:S(2)}) collective-permute-start(bf16[640,640]{1,0:T(8,128)(2,1)S(1)} %get-tuple-element.36), channel_id=1, source_target_pairs={{0,1},{1,2},{2,3},{3,0},{4,5},{5,6},{6,7},{7,4},{8,9},{9,10},{10,1... | collective-permute-start | bytes 2457608 | tf_op jit(solution)/shard_map/ppermute | solution.py:398
  26.7 92.7 %collective-permute-start.19 = (bf16[640,640]{1,0:T(8,128)(2,1)S(1)}, bf16[640,640]{1,0:T(8,128)(2,1)S(1)}, u32[]{:S(2)}, u32[]{:S(2)}) collective-permute-start(bf16[640,640]{1,0:T(8,128)(2,1)S(1)} %get-tuple-element.35), channel_id=1, source_target_pairs={{0,3},{1,0},{2,1},{3,2},{4,7},{5,4},{6,5},{7,6},{8,11},{9,8},{10,9... | collective-permute-start | bytes 2457608 | tf_op jit(solution)/shard_map/ppermute | solution.py:398
  36.1 17.0 %collective-permute-start.5 = (bf16[4,272,256]{2,1,0:T(8,128)(2,1)S(1)}, bf16[4,272,256]{2,1,0:T(8,128)(2,1)S(1)}, u32[]{:S(2)}, u32[]{:S(2)}) collective-permute-start(bf16[4,272,256]{2,1,0:T(8,128)(2,1)S(1)} %broadcast_add_fusion.4), channel_id=1, source_target_pairs={{32,64},{64,96},{96,128},{128,160},{160,192},{192,224},{33,65},{65... | collective-permute-start | bytes 1671176 | tf_op jit(solution)/shard_map/ppermute | solution.py:450
  38.3 17.2 %collective-permute-start.9 = (bf16[4,272,256]{2,1,0:T(8,128)(2,1)S(1)}, bf16[4,272,256]{2,1,0:T(8,128)(2,1)S(1)}, u32[]{:S(2)}, u32[]{:S(2)}) collective-permute-start(bf16[4,272,256]{2,1,0:T(8,128)(2,1)S(1)} %broadcast_add_fusion.3), channel_id=1, source_target_pairs={{224,192},{0,224},{32,0},{64,32},{225,193},{1,225},{33,1},{65,33},... | collective-permute-start | bytes 1671176 | tf_op jit(solution)/shard_map/ppermute | solution.py:451
  42.8 79.2 %collective-permute-start.23 = (bf16[640,640]{1,0:T(8,128)(2,1)S(1)}, bf16[640,640]{1,0:T(8,128)(2,1)S(1)}, u32[]{:S(2)}, u32[]{:S(2)}) collective-permute-start(bf16[640,640]{1,0:T(8,128)(2,1)S(1)} %carve.1), channel_id=1, source_target_pairs={{0,2},{1,3},{2,0},{3,1},{4,6},{5,7},{6,4},{7,5},{8,10},{9,11},{10,... | collective-permute-start | bytes 2457608 | tf_op jit(solution)/shard_map/ppermute | solution.py:398
  53.0 13.9 %collective-permute-start.6 = (bf16[4,272,256]{2,1,0:T(8,128)(2,1)S(1)}, bf16[4,272,256]{2,1,0:T(8,128)(2,1)S(1)}, u32[]{:S(2)}, u32[]{:S(2)}) collective-permute-start(bf16[4,272,256]{2,1,0:T(8,128)(2,1)S(1)} %collective-permute-done.5.refs_0_), channel_id=1, source_target_pairs={{64,96},{96,128},{128,160},{160,192},{192,224},{65,97},{97,129},{1... | collective-permute-start | bytes 1671176 | tf_op jit(solution)/shard_map/ppermute | solution.py:450
  55.5 12.9 %collective-permute-start.10 = (bf16[4,272,256]{2,1,0:T(8,128)(2,1)S(1)}, bf16[4,272,256]{2,1,0:T(8,128)(2,1)S(1)}, u32[]{:S(2)}, u32[]{:S(2)}) collective-permute-start(bf16[4,272,256]{2,1,0:T(8,128)(2,1)S(1)} %collective-permute-done.9.refs_1_), channel_id=1, source_target_pairs={{192,160},{224,192},{0,224},{32,0},{193,161},{225,193},{1,225},{33... | collective-permute-start | bytes 1671176 | tf_op jit(solution)/shard_map/ppermute | solution.py:451
  67.0 13.1 %collective-permute-start.7 = (bf16[2,272,256]{2,1,0:T(8,128)(2,1)S(1)}, bf16[2,272,256]{2,1,0:T(8,128)(2,1)S(1)}, u32[]{:S(2)}, u32[]{:S(2)}) collective-permute-start(bf16[2,272,256]{2,1,0:T(8,128)(2,1)S(1)} %slice.8.refs_3_), channel_id=1, source_target_pairs={{96,128},{128,160},{160,192},{192,224},{97,129},{129,161},{161,193... | collective-permute-start | bytes 835592 | tf_op jit(solution)/shard_map/ppermute | solution.py:482
  68.3 11.8 %collective-permute-start.11 = (bf16[2,272,256]{2,1,0:T(8,128)(2,1)S(1)}, bf16[2,272,256]{2,1,0:T(8,128)(2,1)S(1)}, u32[]{:S(2)}, u32[]{:S(2)}) collective-permute-start(bf16[2,272,256]{2,1,0:T(8,128)(2,1)S(1)} %slice.9.refs_4_), channel_id=1, source_target_pairs={{160,128},{192,160},{224,192},{0,224},{161,129},{193,161},{225,193... | collective-permute-start | bytes 835592 | tf_op jit(solution)/shard_map/ppermute | solution.py:483
  84.8 35.6 %collective-permute-start.12 = (bf16[5,144,256]{2,1,0:T(8,128)(2,1)S(1)}, bf16[5,144,256]{2,1,0:T(8,128)(2,1)S(1)}, u32[]{:S(2)}, u32[]{:S(2)}) collective-permute-start(bf16[5,144,256]{2,1,0:T(8,128)(2,1)S(1)} %get-tuple-element.28), channel_id=1, source_target_pairs={{0,4},{4,0},{1,5},{5,1},{2,6},{6,2},{3,7},{7,3},{8,12},{12,8},{9,1... | collective-permute-start | bytes 1105928 | tf_op jit(solution)/shard_map/ppermute | solution.py:398
  119.2 7.2 %collective-permute-start.18 = (bf16[640,640]{1,0:T(8,128)(2,1)S(1)}, bf16[640,640]{1,0:T(8,128)(2,1)S(1)}, u32[]{:S(2)}, u32[]{:S(2)}) collective-permute-start(bf16[640,640]{1,0:T(8,128)(2,1)S(1)} %broadcast_add_fusion.2.up_w_0_), channel_id=1, source_target_pairs={{0,4},{4,0},{1,5},{5,1},{2,6},{6,2},{3,7},{7,3},{8,12},{12,8},{9,1... | collective-permute-start | bytes 2457608 | tf_op jit(solution)/shard_map/ppermute | solution.py:398
  119.4 7.1 %collective-permute-start.20 = (bf16[640,640]{1,0:T(8,128)(2,1)S(1)}, bf16[640,640]{1,0:T(8,128)(2,1)}, u32[]{:S(2)}, u32[]{:S(2)}) collective-permute-start(bf16[640,640]{1,0:T(8,128)(2,1)S(1)} %broadcast_add_fusion.1.down_w_0_), channel_id=1, source_target_pairs={{0,4},{4,0},{1,5},{5,1},{2,6},{6,2},{3,7},{7,3},{8,12},{12,8},{9,1... | collective-permute-start | bytes 2457608 | tf_op jit(solution)/shard_map/ppermute | solution.py:398
  122.1 17.0 %collective-permute-start.24 = (bf16[640,640]{1,0:T(8,128)(2,1)S(1)}, bf16[640,640]{1,0:T(8,128)(2,1)}, u32[]{:S(2)}, u32[]{:S(2)}) collective-permute-start(bf16[640,640]{1,0:T(8,128)(2,1)S(1)} %broadcast_add_fusion.far_w_0_), channel_id=1, source_target_pairs={{0,4},{4,0},{1,5},{5,1},{2,6},{6,2},{3,7},{7,3},{8,12},{12,8},{9,1... | collective-permute-start | bytes 2457608 | tf_op jit(solution)/shard_map/ppermute | solution.py:398
  122.6 7.6 %collective-permute-start.13 = (bf16[128,640]{1,0:T(8,128)(2,1)S(1)}, bf16[128,640]{1,0:T(8,128)(2,1)}, u32[]{:S(2)}, u32[]{:S(2)}) collective-permute-start(bf16[128,640]{1,0:T(8,128)(2,1)S(1)} %get-tuple-element.29.own_0_), channel_id=1, source_target_pairs={{0,1},{1,2},{2,3},{3,0},{4,5},{5,6},{6,7},{7,4},{8,9},{9,10},{10,1... | collective-permute-start | bytes 491528 | tf_op jit(solution)/shard_map/ppermute | solution.py:398
  126.5 9.3 %collective-permute-start.14 = (bf16[128,640]{1,0:T(8,128)(2,1)}, bf16[128,640]{1,0:T(8,128)(2,1)S(1)}, u32[]{:S(2)}, u32[]{:S(2)}) collective-permute-start(bf16[128,640]{1,0:T(8,128)(2,1)} %get-tuple-element.30.own_1_), channel_id=1, source_target_pairs={{0,1},{1,2},{2,3},{3,0},{4,5},{5,6},{6,7},{7,4},{8,9},{9,10},{10,1... | collective-permute-start | bytes 491528 | tf_op jit(solution)/shard_map/ppermute | solution.py:398
  126.6 9.2 %collective-permute-start.15 = (bf16[128,640]{1,0:T(8,128)(2,1)S(1)}, bf16[128,640]{1,0:T(8,128)(2,1)S(1)}, u32[]{:S(2)}, u32[]{:S(2)}) collective-permute-start(bf16[128,640]{1,0:T(8,128)(2,1)S(1)} %get-tuple-element.29.own_0_), channel_id=1, source_target_pairs={{0,3},{1,0},{2,1},{3,2},{4,7},{5,4},{6,5},{7,6},{8,11},{9,8},{10,9... | collective-permute-start | bytes 491528 | tf_op jit(solution)/shard_map/ppermute | solution.py:398
  130.1 8.9 %collective-permute-start.21 = (bf16[128,640]{1,0:T(8,128)(2,1)}, bf16[128,640]{1,0:T(8,128)(2,1)S(1)}, u32[]{:S(2)}, u32[]{:S(2)}) collective-permute-start(bf16[128,640]{1,0:T(8,128)(2,1)} %collective-permute-done.13.below_0_), channel_id=1, source_target_pairs={{0,1},{1,2},{2,3},{3,0},{4,5},{5,6},{6,7},{7,4},{8,9},{9,10},{10,1... | collective-permute-start | bytes 491528 | tf_op jit(solution)/shard_map/ppermute | solution.py:398
  130.1 8.9 %collective-permute-start.22 = (bf16[128,640]{1,0:T(8,128)(2,1)}, bf16[128,640]{1,0:T(8,128)(2,1)S(1)}, u32[]{:S(2)}, u32[]{:S(2)}) collective-permute-start(bf16[128,640]{1,0:T(8,128)(2,1)} %collective-permute-done.16.above_1_), channel_id=1, source_target_pairs={{0,3},{1,0},{2,1},{3,2},{4,7},{5,4},{6,5},{7,6},{8,11},{9,8},{10,9... | collective-permute-start | bytes 491528 | tf_op jit(solution)/shard_map/ppermute | solution.py:398
  (5 other events, 50.3 us)
